TPU v7x, 32 devices: a whole 2x2x4 slice. The times are simulated.
32 devices in a mesh: blk: 4 (over y, x), grp: 8 (over z, core).
Axes of the slice: x: 2, y: 2, z: 4, core: 2. Of those that a mesh axis runs over, the one named last changes fastest.
Arguments:
- centres: float32 [3, 32768], P(None, ('blk', 'grp')), may hold values from -8 to 8, as said below
- coeffs: float32 [3, 32768], P(None, ('blk', 'grp')), may hold values from -2 to 5.5
- residual: float32 [3, 32768], P(None, ('blk', 'grp')), may hold values from -18 to 18
- direction_prev: float32 [3, 32768], P(None, ('blk', 'grp')), may hold values from -6 to 6
- smoothing: float32 [32768], P(('blk', 'grp')), may hold values from 0.5 to 5
- norm_prev: float32 [3], replicated, may hold values from 32768 to 131072
- support_radius: int32 [1], replicated, may hold values from 900 to 960
- volume_nodes: float32 [3, 32768], P(None, ('blk', 'grp')), may hold values from -10 to 10
- block_lists: int32 [32, 4], P(('blk', 'grp')), may hold values from 0 to 7, as said below
Outputs:
- coeffs_next: float32 [3, 32768], P(None, ('blk', 'grp'))
- residual_next: float32 [3, 32768], P(None, ('blk', 'grp'))
- direction: float32 [3, 32768], P(None, ('blk', 'grp'))
- norm_next: float32 [3], replicated
- displacement: float32 [3, 32768], P(None, ('blk', 'grp'))
Inputs may be any that keep to these rules, and one draw needn't show every extreme that they name: `centres`: every centre of block k has its distance from the z axis within [g, g + 1) with g = k mod 8, and lies at height -0.01 times the square of that distance. `block_lists`: each row names 4 different bands.
All inputs are finite; a program needn't handle non-finite values.
Results may differ from a plain program's by a relative error of at most 0.0003.
Values sent between devices are 32-bit elements; how exact they have to be, the bound alone decides.
A program may use at most 64 MiB of HBM per device.

v0:
```python
import jax
import jax.numpy as jnp
from jax import lax
from jax.sharding import PartitionSpec as P

RADIUS_UNIT = 0.001


def extended(shard, sides, width):
    for axis, dim in sides:
        size, length = (lax.axis_size(axis), shard.shape[dim])
        up = [(i, (i + 1) % size) for i in range(size - 1)]
        down = [(j, i) for i, j in up]
        last = lax.slice_in_dim(shard, length - width, length, axis=dim)
        leading = lax.slice_in_dim(shard, 0, width, axis=dim)
        before = lax.ppermute(last, axis, up)
        after = lax.ppermute(leading, axis, down)
        shard = jnp.concatenate([before, shard, after], axis=dim)
    return shard


def wendland(sources, targets, radius):
    apart_first = sources[0][:, None] - targets[0][None, :]
    apart_second = sources[1][:, None] - targets[1][None, :]
    apart_third = sources[2][:, None] - targets[2][None, :]
    distance = jnp.sqrt(
        apart_first * apart_first + apart_second * apart_second + apart_third * apart_third
    )
    scaled = distance / radius
    remain = jnp.maximum(1.0 - scaled, 0.0)
    square = remain * remain
    return square * square * (4.0 * scaled + 1.0)


def apply_blocks(total, piece, targets, count, radius):
    blocks = piece.shape[1] // count

    def one(index, carry):
        block = lax.dynamic_slice_in_dim(piece, index * count, count, 1)
        weights = wendland(block[:3], targets, radius)
        return carry + jnp.dot(
            block[3:], weights, preferred_element_type=jnp.float32, precision=lax.Precision.HIGHEST
        )

    return lax.fori_loop(0, blocks, one, total)


def per_device(
    centres,
    coeffs,
    residual,
    direction_prev,
    smoothing,
    norm_prev,
    support_radius,
    volume_nodes,
    block_lists,
):
    radius = support_radius[0].astype(jnp.float32) * RADIUS_UNIT
    count = centres.shape[1]
    scaling = 1.0 + smoothing
    precond = residual / scaling
    norm_now = lax.psum(jnp.sum(residual * precond, axis=1), ("blk", "grp"))
    beta = norm_now / norm_prev
    direction = precond + beta[:, None] * direction_prev
    bundle = jnp.concatenate([centres, direction], axis=0)
    widened = extended(bundle, (("grp", 1),), count)
    kernel_part = apply_blocks(
        jnp.zeros((3, count), jnp.float32),
        lax.all_gather(widened, "blk", axis=1, tiled=True),
        centres,
        count,
        radius,
    )
    image = smoothing * direction + kernel_part
    weighted = image / scaling
    curvature, cross, square = lax.psum(
        (
            jnp.sum(direction * image, axis=1),
            jnp.sum(residual * weighted, axis=1),
            jnp.sum(image * weighted, axis=1),
        ),
        ("blk", "grp"),
    )
    alpha = norm_now / curvature
    coeffs_next = coeffs + alpha[:, None] * direction
    residual_next = residual - alpha[:, None] * image
    norm_next = norm_now - 2.0 * alpha * cross + alpha * alpha * square
    stacked = jnp.concatenate([centres, coeffs_next], axis=0)
    listed = block_lists[0]
    empty = jnp.zeros((3, volume_nodes.shape[1]), jnp.float32)

    def contribution(carry, block):
        weights = wendland(block[:3], volume_nodes, radius)
        return carry + jnp.dot(
            block[3:], weights, preferred_element_type=jnp.float32, precision=lax.Precision.HIGHEST
        )

    sector_bands = lax.all_gather(stacked, "grp", axis=1, tiled=True)

    def one_entry(carry, band):
        block = lax.dynamic_slice_in_dim(sector_bands, band * count, count, 1)
        return (contribution(carry, block), None)

    displacement, _ = lax.scan(one_entry, empty, listed)
    return (coeffs_next, residual_next, direction, norm_next, displacement)


def solution(mesh):
    placed = (
        P(None, ("blk", "grp")),
        P(None, ("blk", "grp")),
        P(None, ("blk", "grp")),
        P(None, ("blk", "grp")),
        P(("blk", "grp")),
        P(),
        P(),
        P(None, ("blk", "grp")),
        P(("blk", "grp"), None),
    )
    return jax.shard_map(
        per_device,
        mesh=mesh,
        in_specs=placed,
        out_specs=(
            P(None, ("blk", "grp")),
            P(None, ("blk", "grp")),
            P(None, ("blk", "grp")),
            P(),
            P(None, ("blk", "grp")),
        ),
        check_vma=False,
    )
```

profile of v0, /device:TPU:1, one launch (start us, length us, event | category | flops | bytes accessed | tf_op | source)
XLA Modules:
  0.0 212.0 jit_solution(2917073200692337855)
XLA Ops:
  0.6 0.7 broadcast_add_fusion
  1.3 0.8 multiply_reduce_fusion.3
  2.2 40.6 %psum.28 = f32[3]{0:T(128)S(1)} all-reduce(f32[3]{0:T(128)S(1)} %multiply_reduce_fusion.3), channel_id=1, replica_groups=mesh['blk'=4,'grp'=8] {'blk','grp'}, use_global_device_ids=true, to_apply=%region_1.0 | all-reduce | flops 3 | bytes 24 | tf_op jit(solution)/shard_map/psum | solution.py:63
  42.8 0.7 div.42
  43.4 0.8 multiply_add_fusion.2
  44.2 0.8 pad_maximum_fusion.2
  45.0 4.5 %collective-permute-start = (f32[6,1024]{1,0:T(8,128)S(1)}, f32[6,1024]{1,0:T(8,128)S(1)}, u32[]{:S(2)}, u32[]{:S(2)}) collective-permute-start(f32[6,1024]{1,0:T(8,128)S(1)} %pad_maximum_fusion.2), channel_id=1, source_target_pairs={{0,1},{1,2},{2,3},{3,4},{4,5},{5,6},{6,7},{8,9},{9,10},{10,11},{11... | collective-permute-start | bytes 73736 | tf_op jit(solution)/shard_map/ppermute | solution.py:16
  49.5 1.9 collective-permute-start.1
  52.2 2.6 %collective-permute-done.1 = f32[6,1024]{1,0:T(8,128)S(1)} collective-permute-done((f32[6,1024]{1,0:T(8,128)S(1)}, f32[6,1024]{1,0:T(8,128)S(1)}, u32[]{:S(2)}, u32[]{:S(2)}) %collective-permute-start.1) | collective-permute-done | bytes 24608 | tf_op jit(solution)/shard_map/ppermute | solution.py:17
  54.8 0.7 pad_maximum_fusion
  55.5 8.5 %all_gather.6 = f32[6,12288]{1,0:T(8,128)S(1)} all-gather(f32[6,3072]{1,0:T(8,128)S(1)} %pad_maximum_fusion), channel_id=1, replica_groups=mesh['blk'=4,'grp'=8] {'blk'}, dimensions={1}, use_global_device_ids=true | all-gather | bytes 368640 | tf_op jit(solution)/shard_map/all_gather | solution.py:70
  64.1 64.5 %while.25 = (s32[]{:T(128)}, f32[3,1024]{1,0:T(4,128)S(1)}, f32[6,12288]{1,0:T(8,128)S(1)}, f32[3,1024]{1,0:T(4,128)S(1)}, f32[]{:T(128)}, /*index=5*/s32[]{:T(1...) while((s32[]{:T(128)}, f32[3,1024]{1,0:T(4,128)S(1)}, ...), condition=%wide.region_3.0_spmd.clone, body=%wide.region_2.0_spmd.clone.sunk | while | flops 54532104 | bytes 119017 | solution.py:45
  64.1 0.1 constant_dynamic-slice_fusion.4
  64.2 5.3 %fusion.60 = f32[3,1024]{1,0:T(4,128)S(1)} fusion(f32[]{:T(128)} %get-tuple-element.343, f32[1024]{0:T(1024)S(1)} %bitcast.45, f32[1024]{0:T(1024)S(1)} %bitcast.43, f32[1024]{0:T(1024)S(1)} %bitcast.44, f32[1024]{0:T(1024)S(1)} %bitcast.42, f32[1024]{0:T(1024)S(1)} %bitcast.46, f32[1024]{0:T(1024)S(1)} %bitcast.41, ...), kind=kOutput, calls=%fused_computation.19.clone.1 | convolution fusion | flops 54532096 | bytes 69645 | tf_op jit(solution)/shard_map/while/body/eval_jaxpr/dot_general | solution.py:41
  69.5 0.1 constant_dynamic-slice_fusion.4
  69.6 5.3 %fusion.60 = f32[3,1024]{1,0:T(4,128)S(1)} fusion(f32[]{:T(128)} %get-tuple-element.343, f32[1024]{0:T(1024)S(1)} %bitcast.45, f32[1024]{0:T(1024)S(1)} %bitcast.43, f32[1024]{0:T(1024)S(1)} %bitcast.44, f32[1024]{0:T(1024)S(1)} %bitcast.42, f32[1024]{0:T(1024)S(1)} %bitcast.46, f32[1024]{0:T(1024)S(1)} %bitcast.41, ...), kind=kOutput, calls=%fused_computation.19.clone.1 | convolution fusion | flops 54532096 | bytes 69645 | tf_op jit(solution)/shard_map/while/body/eval_jaxpr/dot_general | solution.py:41
  74.8 0.1 constant_dynamic-slice_fusion.4
  74.9 5.3 %fusion.60 = f32[3,1024]{1,0:T(4,128)S(1)} fusion(f32[]{:T(128)} %get-tuple-element.343, f32[1024]{0:T(1024)S(1)} %bitcast.45, f32[1024]{0:T(1024)S(1)} %bitcast.43, f32[1024]{0:T(1024)S(1)} %bitcast.44, f32[1024]{0:T(1024)S(1)} %bitcast.42, f32[1024]{0:T(1024)S(1)} %bitcast.46, f32[1024]{0:T(1024)S(1)} %bitcast.41, ...), kind=kOutput, calls=%fused_computation.19.clone.1 | convolution fusion | flops 54532096 | bytes 69645 | tf_op jit(solution)/shard_map/while/body/eval_jaxpr/dot_general | solution.py:41
  80.2 0.1 constant_dynamic-slice_fusion.4
  80.3 5.3 %fusion.60 = f32[3,1024]{1,0:T(4,128)S(1)} fusion(f32[]{:T(128)} %get-tuple-element.343, f32[1024]{0:T(1024)S(1)} %bitcast.45, f32[1024]{0:T(1024)S(1)} %bitcast.43, f32[1024]{0:T(1024)S(1)} %bitcast.44, f32[1024]{0:T(1024)S(1)} %bitcast.42, f32[1024]{0:T(1024)S(1)} %bitcast.46, f32[1024]{0:T(1024)S(1)} %bitcast.41, ...), kind=kOutput, calls=%fused_computation.19.clone.1 | convolution fusion | flops 54532096 | bytes 69645 | tf_op jit(solution)/shard_map/while/body/eval_jaxpr/dot_general | solution.py:41
  85.6 0.1 constant_dynamic-slice_fusion.4
  85.7 5.3 %fusion.60 = f32[3,1024]{1,0:T(4,128)S(1)} fusion(f32[]{:T(128)} %get-tuple-element.343, f32[1024]{0:T(1024)S(1)} %bitcast.45, f32[1024]{0:T(1024)S(1)} %bitcast.43, f32[1024]{0:T(1024)S(1)} %bitcast.44, f32[1024]{0:T(1024)S(1)} %bitcast.42, f32[1024]{0:T(1024)S(1)} %bitcast.46, f32[1024]{0:T(1024)S(1)} %bitcast.41, ...), kind=kOutput, calls=%fused_computation.19.clone.1 | convolution fusion | flops 54532096 | bytes 69645 | tf_op jit(solution)/shard_map/while/body/eval_jaxpr/dot_general | solution.py:41
  91.0 5.3 %fusion.60 = f32[3,1024]{1,0:T(4,128)S(1)} fusion(f32[]{:T(128)} %get-tuple-element.343, f32[1024]{0:T(1024)S(1)} %bitcast.45, f32[1024]{0:T(1024)S(1)} %bitcast.43, f32[1024]{0:T(1024)S(1)} %bitcast.44, f32[1024]{0:T(1024)S(1)} %bitcast.42, f32[1024]{0:T(1024)S(1)} %bitcast.46, f32[1024]{0:T(1024)S(1)} %bitcast.41, ...), kind=kOutput, calls=%fused_computation.19.clone.1 | convolution fusion | flops 54532096 | bytes 69645 | tf_op jit(solution)/shard_map/while/body/eval_jaxpr/dot_general | solution.py:41
  96.4 5.3 %fusion.60 = f32[3,1024]{1,0:T(4,128)S(1)} fusion(f32[]{:T(128)} %get-tuple-element.343, f32[1024]{0:T(1024)S(1)} %bitcast.45, f32[1024]{0:T(1024)S(1)} %bitcast.43, f32[1024]{0:T(1024)S(1)} %bitcast.44, f32[1024]{0:T(1024)S(1)} %bitcast.42, f32[1024]{0:T(1024)S(1)} %bitcast.46, f32[1024]{0:T(1024)S(1)} %bitcast.41, ...), kind=kOutput, calls=%fused_computation.19.clone.1 | convolution fusion | flops 54532096 | bytes 69645 | tf_op jit(solution)/shard_map/while/body/eval_jaxpr/dot_general | solution.py:41
  101.8 5.3 %fusion.60 = f32[3,1024]{1,0:T(4,128)S(1)} fusion(f32[]{:T(128)} %get-tuple-element.343, f32[1024]{0:T(1024)S(1)} %bitcast.45, f32[1024]{0:T(1024)S(1)} %bitcast.43, f32[1024]{0:T(1024)S(1)} %bitcast.44, f32[1024]{0:T(1024)S(1)} %bitcast.42, f32[1024]{0:T(1024)S(1)} %bitcast.46, f32[1024]{0:T(1024)S(1)} %bitcast.41, ...), kind=kOutput, calls=%fused_computation.19.clone.1 | convolution fusion | flops 54532096 | bytes 69645 | tf_op jit(solution)/shard_map/while/body/eval_jaxpr/dot_general | solution.py:41
  107.2 5.3 %fusion.60 = f32[3,1024]{1,0:T(4,128)S(1)} fusion(f32[]{:T(128)} %get-tuple-element.343, f32[1024]{0:T(1024)S(1)} %bitcast.45, f32[1024]{0:T(1024)S(1)} %bitcast.43, f32[1024]{0:T(1024)S(1)} %bitcast.44, f32[1024]{0:T(1024)S(1)} %bitcast.42, f32[1024]{0:T(1024)S(1)} %bitcast.46, f32[1024]{0:T(1024)S(1)} %bitcast.41, ...), kind=kOutput, calls=%fused_computation.19.clone.1 | convolution fusion | flops 54532096 | bytes 69645 | tf_op jit(solution)/shard_map/while/body/eval_jaxpr/dot_general | solution.py:41
  112.5 5.3 %fusion.60 = f32[3,1024]{1,0:T(4,128)S(1)} fusion(f32[]{:T(128)} %get-tuple-element.343, f32[1024]{0:T(1024)S(1)} %bitcast.45, f32[1024]{0:T(1024)S(1)} %bitcast.43, f32[1024]{0:T(1024)S(1)} %bitcast.44, f32[1024]{0:T(1024)S(1)} %bitcast.42, f32[1024]{0:T(1024)S(1)} %bitcast.46, f32[1024]{0:T(1024)S(1)} %bitcast.41, ...), kind=kOutput, calls=%fused_computation.19.clone.1 | convolution fusion | flops 54532096 | bytes 69645 | tf_op jit(solution)/shard_map/while/body/eval_jaxpr/dot_general | solution.py:41
  117.9 5.3 %fusion.60 = f32[3,1024]{1,0:T(4,128)S(1)} fusion(f32[]{:T(128)} %get-tuple-element.343, f32[1024]{0:T(1024)S(1)} %bitcast.45, f32[1024]{0:T(1024)S(1)} %bitcast.43, f32[1024]{0:T(1024)S(1)} %bitcast.44, f32[1024]{0:T(1024)S(1)} %bitcast.42, f32[1024]{0:T(1024)S(1)} %bitcast.46, f32[1024]{0:T(1024)S(1)} %bitcast.41, ...), kind=kOutput, calls=%fused_computation.19.clone.1 | convolution fusion | flops 54532096 | bytes 69645 | tf_op jit(solution)/shard_map/while/body/eval_jaxpr/dot_general | solution.py:41
  123.3 5.3 %fusion.60 = f32[3,1024]{1,0:T(4,128)S(1)} fusion(f32[]{:T(128)} %get-tuple-element.343, f32[1024]{0:T(1024)S(1)} %bitcast.45, f32[1024]{0:T(1024)S(1)} %bitcast.43, f32[1024]{0:T(1024)S(1)} %bitcast.44, f32[1024]{0:T(1024)S(1)} %bitcast.42, f32[1024]{0:T(1024)S(1)} %bitcast.46, f32[1024]{0:T(1024)S(1)} %bitcast.41, ...), kind=kOutput, calls=%fused_computation.19.clone.1 | convolution fusion | flops 54532096 | bytes 69645 | tf_op jit(solution)/shard_map/while/body/eval_jaxpr/dot_general | solution.py:41
  128.6 0.2 multiply_reduce_fusion.1
  128.7 39.1 %all-reduce = (f32[3]{0:T(128)S(1)}, f32[3]{0:T(128)S(1)}, f32[3]{0:T(128)S(1)}) all-reduce(f32[3]{0:T(128)S(1)} %get-tuple-element.174, f32[3]{0:T(128)S(1)} %get-tuple-element.173, f32[3]{0:T(128)S(1)} %get-tuple-element.172), channel_id=1, replica_groups=mesh['blk'=4,'grp'=8] {'blk','grp'}, use_global_device_ids=true, to_apply=%region_5.0 | all-reduce | flops 9 | bytes 72 | tf_op jit(solution)/shard_map/psum | solution.py:77
  167.9 0.5 multiply_add_fusion.3
  168.4 0.7 multiply_subtract_fusion
  169.1 15.7 %all_gather.7 = f32[6,8192]{1,0:T(8,128)S(1)} all-gather(f32[6,1024]{1,0:T(8,128)S(1)} %pad_maximum_fusion.1), channel_id=1, replica_groups=mesh['blk'=4,'grp'=8] {'grp'}, dimensions={1}, use_global_device_ids=true | all-gather | bytes 221184 | tf_op jit(solution)/shard_map/all_gather | solution.py:99
  184.8 26.5 %while.26 = (s32[]{:T(128)}, f32[3,1024]{1,0:T(4,128)S(1)}, s32[4]{0:T(128)S(1)}, f32[6,8192]{1,0:T(8,128)S(1)}, f32[3,1024]{1,0:T(4,128)S(1)}, /*index=5*/f32[]...) while((s32[]{:T(128)}, f32[3,1024]{1,0:T(4,128)S(1)}, ...), condition=%wide.region_11.12_spmd.clone, body=%wide.region_10.11_spmd.clone.sunk | while | flops 54532104 | bytes 119037 | solution.py:105
  184.8 0.6 dynamic_slice.18
  186.1 0.1 constant_dynamic-slice_fusion.5
  186.2 5.3 %fusion.63 = f32[3,1024]{1,0:T(4,128)S(1)} fusion(f32[]{:T(128)} %get-tuple-element.382, f32[1024]{0:T(1024)S(1)} %bitcast.51, f32[1024]{0:T(1024)S(1)} %bitcast.49, f32[1024]{0:T(1024)S(1)} %bitcast.50, f32[1024]{0:T(1024)S(1)} %bitcast.48, f32[1024]{0:T(1024)S(1)} %bitcast.52, f32[1024]{0:T(1024)S(1)} %bitcast.47, ...), kind=kOutput, calls=%fused_computation.44.clone.1 | convolution fusion | flops 54532096 | bytes 69645 | tf_op jit(solution)/shard_map/while/body/eval_jaxpr/dot_general | solution.py:95
  191.5 0.6 dynamic_slice.18
  192.7 0.1 constant_dynamic-slice_fusion.5
  192.8 5.3 %fusion.63 = f32[3,1024]{1,0:T(4,128)S(1)} fusion(f32[]{:T(128)} %get-tuple-element.382, f32[1024]{0:T(1024)S(1)} %bitcast.51, f32[1024]{0:T(1024)S(1)} %bitcast.49, f32[1024]{0:T(1024)S(1)} %bitcast.50, f32[1024]{0:T(1024)S(1)} %bitcast.48, f32[1024]{0:T(1024)S(1)} %bitcast.52, f32[1024]{0:T(1024)S(1)} %bitcast.47, ...), kind=kOutput, calls=%fused_computation.44.clone.1 | convolution fusion | flops 54532096 | bytes 69645 | tf_op jit(solution)/shard_map/while/body/eval_jaxpr/dot_general | solution.py:95
  198.1 0.6 dynamic_slice.18
  199.3 0.1 constant_dynamic-slice_fusion.5
  199.4 5.3 %fusion.63 = f32[3,1024]{1,0:T(4,128)S(1)} fusion(f32[]{:T(128)} %get-tuple-element.382, f32[1024]{0:T(1024)S(1)} %bitcast.51, f32[1024]{0:T(1024)S(1)} %bitcast.49, f32[1024]{0:T(1024)S(1)} %bitcast.50, f32[1024]{0:T(1024)S(1)} %bitcast.48, f32[1024]{0:T(1024)S(1)} %bitcast.52, f32[1024]{0:T(1024)S(1)} %bitcast.47, ...), kind=kOutput, calls=%fused_computation.44.clone.1 | convolution fusion | flops 54532096 | bytes 69645 | tf_op jit(solution)/shard_map/while/body/eval_jaxpr/dot_general | solution.py:95
  204.7 0.6 dynamic_slice.18
  206.0 0.1 constant_dynamic-slice_fusion.5
  206.1 5.3 %fusion.63 = f32[3,1024]{1,0:T(4,128)S(1)} fusion(f32[]{:T(128)} %get-tuple-element.382, f32[1024]{0:T(1024)S(1)} %bitcast.51, f32[1024]{0:T(1024)S(1)} %bitcast.49, f32[1024]{0:T(1024)S(1)} %bitcast.50, f32[1024]{0:T(1024)S(1)} %bitcast.48, f32[1024]{0:T(1024)S(1)} %bitcast.52, f32[1024]{0:T(1024)S(1)} %bitcast.47, ...), kind=kOutput, calls=%fused_computation.44.clone.1 | convolution fusion | flops 54532096 | bytes 69645 | tf_op jit(solution)/shard_map/while/body/eval_jaxpr/dot_general | solution.py:95
  211.3 0.6 copy-done.8
  (28 shorter events, 0.7 us)
Async XLA Ops:
  44.2 124.2 %copy-start.1 = (f32[3,1024]{1,0:T(4,128)}, f32[3,1024]{1,0:T(4,128)S(1)}, u32[]{:S(2)}) copy-start(f32[3,1024]{1,0:T(4,128)S(1)} %multiply_add_fusion.2) | copy-start | bytes 36868
  44.2 19.8 %copy-start = (f32[3,1024]{1,0:T(4,128)S(1)}, f32[3,1024]{1,0:T(4,128)}, u32[]{:S(2)}) copy-start(f32[3,1024]{1,0:T(4,128)} %param.13) | copy-start | bytes 36868
  45.0 7.1 %collective-permute-start = (f32[6,1024]{1,0:T(8,128)S(1)}, f32[6,1024]{1,0:T(8,128)S(1)}, u32[]{:S(2)}, u32[]{:S(2)}) collective-permute-start(f32[6,1024]{1,0:T(8,128)S(1)} %pad_maximum_fusion.2), channel_id=1, source_target_pairs={{0,1},{1,2},{2,3},{3,4},{4,5},{5,6},{6,7},{8,9},{9,10},{10,11},{11... | collective-permute-start | bytes 73736 | tf_op jit(solution)/shard_map/ppermute | solution.py:16
  49.5 5.2 %collective-permute-start.1 = (f32[6,1024]{1,0:T(8,128)S(1)}, f32[6,1024]{1,0:T(8,128)S(1)}, u32[]{:S(2)}, u32[]{:S(2)}) collective-permute-start(f32[6,1024]{1,0:T(8,128)S(1)} %pad_maximum_fusion.2), channel_id=1, source_target_pairs={{1,0},{2,1},{3,2},{4,3},{5,4},{6,5},{7,6},{9,8},{10,9},{11,10},{12... | collective-permute-start | bytes 73736 | tf_op jit(solution)/shard_map/ppermute | solution.py:17
  64.0 64.5 %copy-start.2 = (f32[3,1024]{1,0:T(4,128)S(1)}, f32[3,1024]{1,0:T(4,128)}, u32[]{:S(2)}) copy-start(f32[3,1024]{1,0:T(4,128)} %param.15) | copy-start | bytes 36868
  64.1 64.5 %copy-start.5 = (f32[1024]{0:T(1024)S(1)}, f32[1024]{0:T(1024)}, u32[]{:S(2)}) copy-start(f32[1024]{0:T(1024)} %param.17) | copy-start | bytes 12292
  64.1 104.3 %copy-start.6 = (f32[3,1024]{1,0:T(4,128)S(1)}, f32[3,1024]{1,0:T(4,128)}, u32[]{:S(2)}) copy-start(f32[3,1024]{1,0:T(4,128)} %param.14) | copy-start | bytes 36868
  128.5 56.3 %copy-start.3 = (f32[3,1024]{1,0:T(4,128)S(1)}, f32[3,1024]{1,0:T(4,128)}, u32[]{:S(2)}) copy-start(f32[3,1024]{1,0:T(4,128)} %param.20) | copy-start | bytes 36868
  128.5 56.3 %copy-start.7 = (s32[1,4]{1,0:T(1,128)S(1)}, s32[1,4]{1,0:T(1,128)}, u32[]{:S(2)}) copy-start(s32[1,4]{1,0:T(1,128)} %param.21) | copy-start | bytes 52
  169.1 15.7 %copy-start.4 = (f32[3,1024]{1,0:T(4,128)}, f32[3,1024]{1,0:T(4,128)S(1)}, u32[]{:S(2)}) copy-start(f32[3,1024]{1,0:T(4,128)S(1)} %get-tuple-element.222) | copy-start | bytes 36868
  211.3 0.6 copy-start.8
where the time goes:
time: 213 us; the launch traced here: 212 us
  blocking collectives  104 us (49%)
  matrix products  84.4 us (40%)
  starting transfers between devices  6.42 us (3%)
  other arithmetic  5.92 us (3%)
  local copies, waits for them, and re-layouts  4.62 us (2%)
  waiting for transfers between devices  2.63 us (1%)
  loops' own time  2.63 us (1%)
    dot_general x12, matrix products, one(): jnp.dot(block[3:], weights, preferred_element_type=jnp.float32, precision...  63.3 us
    psum x1, blocking collectives, per_device(): norm_now = lax.psum(jnp.sum(residual * precond, axis=1), ('blk', 'grp'))  40.6 us
    psum x1, blocking collectives, per_device(): lax.psum((jnp.sum(direction * image, axis=1), jnp.sum(residual * weighted...  39.1 us
    dot_general x4, matrix products, contribution(): jnp.dot(block[3:], weights, preferred_element_type=jnp.float32, precision...  21.1 us
    all_gather x1, blocking collectives, per_device(): sector_bands = lax.all_gather(stacked, 'grp', axis=1, tiled=True)  15.7 us
    all_gather x1, blocking collectives, per_device(): lax.all_gather(widened, 'blk', axis=1, tiled=True)  8.53 us
    ppermute x1, starting transfers between devices, extended(): before = lax.ppermute(last, axis, up)  4.5 us
  transfers between devices with their start and end apart: 2, of which 1 were waited for; matrix products, arithmetic and copies ran while one was open for 0% of the time, Pallas kernels for 0%

commit v1 on v0

v1 whole, which is shorter than its diff:
```python
import functools
import jax
import jax.numpy as jnp
from jax import lax
from jax.experimental import pallas as pl
from jax.experimental.pallas import tpu as pltpu
from jax.sharding import PartitionSpec as P

RADIUS_UNIT = 0.001
CURVE = 0.01
F32 = jnp.float32
BF16 = jnp.bfloat16
MESH = pl.DeviceIdType.MESH


def rounded(value):
    return value.astype(BF16).astype(F32)


def pieces(coords):
    high = jnp.floor(coords * 4.0 + 0.5) * 0.25
    rest = coords - high
    low = rounded(rest)
    lower = rounded(rest - low)
    big = jnp.sum(high * high, axis=0, keepdims=True)
    small = jnp.sum(rest * (2.0 * high + rest), axis=0, keepdims=True)
    big_a = rounded(big)
    small_a = rounded(small)
    small_b = rounded(small - small_a)
    return high, low, lower, (big_a, big - big_a), (small_a, small_b, small - small_a - small_b)


def rows_of(base, row, first, values):
    for index, value in enumerate(values):
        base = jnp.where(row == first + index, value, base)
    return base


def source_factor(coords, row):
    high, low, lower, big, small = pieces(coords)
    one = 1.0
    return jnp.concatenate(
        [
            rows_of(high, row, 3, big + (one, one)),
            rows_of(low, row, 3, small),
            rows_of(lower, row, 3, (one, one, one)),
            high,
            high,
            low,
            lower,
            low,
        ],
        axis=0,
    ).astype(BF16)


def target_factor(coords, row):
    high, low, lower, big, small = pieces(coords)
    high, low, lower = -2.0 * high, -2.0 * low, -2.0 * lower
    one = 1.0
    return jnp.concatenate(
        [
            rows_of(high, row, 3, (one, one) + big),
            rows_of(high, row, 3, (one, one, one)),
            rows_of(high, row, 3, small),
            low,
            lower,
            low,
            low,
            lower,
        ],
        axis=0,
    )


def kernel(
    blk,
    grp,
    centres,
    coeffs,
    residual,
    direction_prev,
    smoothing,
    norm_prev,
    support_radius,
    nodes,
    lists,
    coeffs_next,
    residual_next,
    direction_out,
    norm_next,
    displacement,
    slots,
    coeff_slots,
    factor_c,
    factor_v,
    factor_s,
    values,
    acc,
    acc_v,
    red_blk,
    red_grp,
    send_sem,
    recv_sem,
    csend_sem,
    crecv_sem,
    bsend_sem,
    brecv_sem,
    gsend_sem,
    grecv_sem,
):
    s = lax.axis_index("blk")
    g = lax.axis_index("grp")
    count = centres.shape[1]
    near = 3 * blk
    tile = 256

    def plan(i):
        k = i % blk
        j = i // blk
        return k, j, jnp.where(j == 1, -1, jnp.where(j == 2, 1, 0))

    def near_copy(i, start):
        k, j, shift = plan(i)
        to_s = lax.rem(s - k + blk, blk)
        to_g = g - shift
        slot = jnp.where(k == 0, g, grp + (k - 1) * 3 + j)

        @pl.when((to_g >= 0) & (to_g < grp))
        def _():
            start(to_s, to_g, slot, i)

    def far_loop(start):
        def step(m, _):
            to_g = lax.rem(g + m, grp)

            @pl.when((to_g - g > 1) | (g - to_g > 1))
            def _():
                start(s, to_g, g, near + m)

            return 0

        lax.fori_loop(1, grp, step, 0)

    def copy_of(to_s, to_g, slot, sem):
        return pltpu.make_async_remote_copy(
            src_ref=slots.at[g],
            dst_ref=slots.at[slot],
            send_sem=send_sem.at[sem],
            recv_sem=recv_sem.at[slot],
            device_id=(to_s, to_g),
            device_id_type=MESH,
        )

    def coeff_copy(m, slot):
        return pltpu.make_async_remote_copy(
            src_ref=coeff_slots.at[g],
            dst_ref=coeff_slots.at[slot],
            send_sem=csend_sem.at[m],
            recv_sem=crecv_sem.at[slot],
            device_id=(s, lax.rem(g + m, grp)),
            device_id_type=MESH,
        )

    barrier = pltpu.get_barrier_semaphore()

    def greet(to_s, to_g, slot, sem):
        pl.semaphore_signal(barrier, inc=1, device_id=(to_s, to_g), device_id_type=MESH)

    def near_loop(start):
        def step(i, _):
            near_copy(i, start)
            return 0

        lax.fori_loop(1, near, step, 0)

    near_loop(greet)
    far_loop(greet)

    weight = 1.0 / (1.0 + smoothing[...])
    precond = residual[...] * weight
    slots[g] = jnp.concatenate(
        [precond, direction_prev[...], centres[0:2, :]], axis=0
    )
    coeff_slots[g] = jnp.concatenate([coeffs[...], jnp.zeros((1, count), F32)], axis=0)

    bands = 3 - jnp.where(g == 0, 1, 0) - jnp.where(g == grp - 1, 1, 0)
    pl.semaphore_wait(barrier, grp - 1 + (blk - 1) * bands)

    near_loop(lambda to_s, to_g, slot, sem: copy_of(to_s, to_g, slot, sem).start())
    far_loop(lambda to_s, to_g, slot, sem: copy_of(to_s, to_g, slot, sem).start())

    def start_coeffs(m, _):
        coeff_copy(m, g).start()
        return 0

    lax.fori_loop(1, grp, start_coeffs, 0)

    radius = support_radius[0].astype(F32) * RADIUS_UNIT
    row = lax.broadcasted_iota(jnp.int32, (8, count), 0)
    gap = jnp.zeros((5, count), F32)
    factor_c[...] = target_factor(jnp.concatenate([centres[...], gap], axis=0), row).T.astype(BF16)
    factor_v[...] = target_factor(jnp.concatenate([nodes[...], gap], axis=0), row).T.astype(BF16)
    acc[...] = jnp.zeros_like(acc)
    acc_v[...] = jnp.zeros_like(acc_v)

    def prepare(block, coeff):
        first = block[6:7, :]
        second = block[7:8, :]
        third = (first * first + second * second) * (-CURVE)
        coords = rows_of(jnp.zeros((8, count), F32), row, 0, (first, second, third))
        factor_s[...] = source_factor(coords, row)
        high = rounded(block)
        parts = [high, block - high]
        if coeff is not None:
            chigh = rounded(coeff)
            parts += [chigh, coeff - chigh, jnp.zeros((8, count), F32)]
        values[0 : 32 if coeff is not None else 16, :] = jnp.concatenate(parts, axis=0).astype(BF16)

    def product(factor, total, rows):
        def step(at, _):
            start = pl.multiple_of(at * tile, tile)
            left = factor[pl.ds(start, tile), :]
            out = jnp.zeros((tile, rows), F32)
            for cut in range(0, count, tile):
                apart = jnp.dot(
                    left, factor_s[:, cut : cut + tile], preferred_element_type=F32
                )
                apart = jnp.maximum(apart, 1e-12)
                remain = jnp.maximum(radius - apart * lax.rsqrt(apart), 0.0)
                square = remain * remain
                weights = square * square * (1.25 * radius - remain)
                whole = weights.astype(BF16)
                part = (weights - whole.astype(F32)).astype(BF16)
                right = values[0:rows, cut : cut + tile]
                contract = (((1,), (1,)), ((), ()))
                out += lax.dot_general(whole, right, contract, preferred_element_type=F32)
                out += lax.dot_general(part, right, contract, preferred_element_type=F32)
            total[pl.ds(start, tile), 0:rows] += out
            return 0

        lax.fori_loop(0, count // tile, step, 0)

    def near_block(i, _):
        k, j, shift = plan(i)
        band = g + shift

        @pl.when((band >= 0) & (band < grp))
        def _():
            slot = jnp.where(k == 0, band, grp + (k - 1) * 3 + j)

            @pl.when(i > 0)
            def _():
                copy_of(s, g, slot, i).wait_recv()

            prepare(slots[slot], None)
            product(factor_c, acc, 16)

        return 0

    lax.fori_loop(0, near, near_block, 0)

    rescale = 4.0 / (radius * radius * radius * radius * radius)
    turned = acc[...].T
    applied = (turned[0:8, :] + turned[8:16, :]) * rescale
    smooth = smoothing[...]
    previous = direction_prev[...]
    image_p = smooth * precond + applied[0:3, :]
    image_d = smooth * previous + applied[3:6, :]
    lane = lax.broadcasted_iota(jnp.int32, (3, 128), 1)
    terms = (
        residual[...] * precond,
        precond * image_p,
        precond * image_d,
        previous * image_p,
        previous * image_d,
        image_p * image_p * weight,
        image_p * image_d * weight,
        image_d * image_d * weight,
    )
    packed = jnp.zeros((3, 128), F32)
    for index, term in enumerate(terms):
        packed = jnp.where(lane == index, jnp.sum(term, axis=1, keepdims=True), packed)
    filled = jnp.concatenate([packed, jnp.zeros((5, 128), F32)], axis=0)

    red_blk[s] = filled

    def blk_copy(m, slot):
        return pltpu.make_async_remote_copy(
            src_ref=red_blk.at[s],
            dst_ref=red_blk.at[slot],
            send_sem=bsend_sem.at[m],
            recv_sem=brecv_sem.at[slot],
            device_id=(lax.rem(s + m, blk), g),
            device_id_type=MESH,
        )

    for m in range(1, blk):
        blk_copy(m, s).start()

    def await_far(to_s, to_g, slot, sem):
        copy_of(s, g, to_g, sem).wait_recv()

    far_loop(await_far)

    def await_coeffs(m, _):
        coeff_copy(m, lax.rem(g + m, grp)).wait_recv()
        return 0

    lax.fori_loop(1, grp, await_coeffs, 0)

    for m in range(1, blk):
        blk_copy(m, lax.rem(s + m, blk)).wait_recv()
    red_grp[g] = jnp.sum(red_blk[...], axis=0)

    def grp_copy(m, slot):
        return pltpu.make_async_remote_copy(
            src_ref=red_grp.at[g],
            dst_ref=red_grp.at[slot],
            send_sem=gsend_sem.at[m],
            recv_sem=grecv_sem.at[slot],
            device_id=(s, lax.rem(g + m, grp)),
            device_id_type=MESH,
        )

    def start_grp(m, _):
        grp_copy(m, g).start()
        return 0

    lax.fori_loop(1, grp, start_grp, 0)

    def listed_block(entry, _):
        band = lists[0, entry]
        prepare(slots[band], coeff_slots[band])
        product(factor_v, acc_v, 32)
        return 0

    lax.fori_loop(0, lists.shape[1], listed_block, 0)

    def await_grp(m, _):
        grp_copy(m, lax.rem(g + m, grp)).wait_recv()
        return 0

    lax.fori_loop(1, grp, await_grp, 0)
    totals = jnp.sum(red_grp[...], axis=0)[0:3, :]
    now, pp, pd, dp, dd, ipp, ipd, idd = (
        jnp.sum(jnp.where(lane == index, totals, 0.0), axis=1, keepdims=True)
        for index in range(8)
    )
    beta = now / norm_prev[:, 0:1]
    curvature = pp + beta * (pd + dp) + beta * beta * dd
    alpha = now / curvature
    cross = pp + beta * pd
    square = ipp + 2.0 * beta * ipd + beta * beta * idd
    norm_next[...] = jnp.broadcast_to(
        now - 2.0 * alpha * cross + alpha * alpha * square, norm_next.shape
    )
    direction = precond + beta * previous
    direction_out[...] = direction
    coeffs_next[...] = coeffs[...] + alpha * direction
    residual_next[...] = residual[...] - alpha * (image_p + beta * image_d)
    turned_v = acc_v[...].T * rescale
    applied_v = turned_v[0:8, :] + turned_v[8:16, :]
    applied_c = turned_v[16:24, :]
    base = applied_c[0:3, :] + applied_c[4:7, :]
    displacement[...] = base + alpha * (applied_v[0:3, :] + beta * applied_v[3:6, :])

    near_loop(lambda to_s, to_g, slot, sem: copy_of(to_s, to_g, slot, sem).wait_send())
    far_loop(lambda to_s, to_g, slot, sem: copy_of(to_s, to_g, slot, sem).wait_send())

    def finish(m, _):
        coeff_copy(m, g).wait_send()
        grp_copy(m, g).wait_send()
        return 0

    lax.fori_loop(1, grp, finish, 0)
    for m in range(1, blk):
        blk_copy(m, s).wait_send()


def per_device(blk, grp, *args):
    (
        centres,
        coeffs,
        residual,
        direction_prev,
        smoothing,
        norm_prev,
        support_radius,
        nodes,
        lists,
    ) = args
    count = centres.shape[1]
    vmem = pl.BlockSpec(memory_space=pltpu.VMEM)
    smem = pl.BlockSpec(memory_space=pltpu.SMEM)
    shape = jax.ShapeDtypeStruct((3, count), F32)
    dma = pltpu.SemaphoreType.DMA
    near = 3 * blk
    slots = grp + 3 * (blk - 1)
    blocks = near + lists.shape[1]
    result = pl.pallas_call(
        functools.partial(kernel, blk, grp),
        out_shape=(
            shape,
            shape,
            shape,
            jax.ShapeDtypeStruct((3, 128), F32),
            jax.ShapeDtypeStruct((3, nodes.shape[1]), F32),
        ),
        in_specs=[vmem, vmem, vmem, vmem, vmem, vmem, smem, vmem, smem],
        out_specs=(vmem,) * 5,
        scratch_shapes=[
            pltpu.VMEM((slots, 8, count), F32),
            pltpu.VMEM((grp, 4, count), F32),
            pltpu.VMEM((count, 64), BF16),
            pltpu.VMEM((nodes.shape[1], 64), BF16),
            pltpu.VMEM((64, count), BF16),
            pltpu.VMEM((32, count), BF16),
            pltpu.VMEM((count, 128), F32),
            pltpu.VMEM((nodes.shape[1], 128), F32),
            pltpu.VMEM((blk, 8, 128), F32),
            pltpu.VMEM((grp, 8, 128), F32),
            dma((near + grp,)),
            dma((slots,)),
            dma((grp,)),
            dma((grp,)),
            dma((blk,)),
            dma((blk,)),
            dma((grp,)),
            dma((grp,)),
        ],
        compiler_params=pltpu.CompilerParams(
            collective_id=0, has_side_effects=True, vmem_limit_bytes=40 * 1024 * 1024
        ),
        cost_estimate=pl.CostEstimate(
            flops=30 * blocks * count * count,
            bytes_accessed=1 << 20,
            transcendentals=blocks * count * count,
        ),
        name="morph_step",
    )(
        centres,
        coeffs,
        residual,
        direction_prev,
        smoothing[None, :],
        jnp.broadcast_to(norm_prev[:, None], (3, 128)),
        support_radius,
        nodes,
        lists,
    )
    coeffs_next, residual_next, direction, norm_next, displacement = result
    return coeffs_next, residual_next, direction, norm_next[:, 0], displacement


def solution(mesh):
    split = P(None, ("blk", "grp"))
    placed = (
        split,
        split,
        split,
        split,
        P(("blk", "grp")),
        P(),
        P(),
        split,
        P(("blk", "grp"), None),
    )
    return jax.shard_map(
        functools.partial(per_device, mesh.shape["blk"], mesh.shape["grp"]),
        mesh=mesh,
        in_specs=placed,
        out_specs=(split, split, split, P(), split),
        check_vma=False,
    )
```

time: 213 us -> 85.8 us (0.40)
  blocking collectives: 104 us -> 0 us
  matrix products: 84.4 us -> 0 us
  Pallas kernels: 0 us -> 76.5 us
  starting transfers between devices: 6.42 us -> 0 us
  other arithmetic: 5.92 us -> 0 us
  local copies, waits for them, and re-layouts: 4.62 us -> 7.37 us
  loops' own time: 2.63 us -> 0 us
  waiting for transfers between devices: 2.63 us -> 0 us
    dot_general x16 -> x0, matrix products: 84.4 us -> none  [the longest x12 63.3 us: one(): jnp.dot(block[3:], weights, preferred_element_type=jnp.float32, precision...]
    psum x2 -> x0, blocking collectives: 79.7 us -> none  [the longest x1 40.6 us: per_device(): norm_now = lax.psum(jnp.sum(residual * precond, axis=1), ('blk', 'grp'))]
    pallas_call x0 -> x1, Pallas kernels: none -> 76.5 us  [per_device(): pl.pallas_call(functools.partial(kernel, blk, grp), out_shape=(shape, sha...]
    all_gather x2 -> x0, blocking collectives: 24.2 us -> none  [the longest x1 15.7 us: per_device(): sector_bands = lax.all_gather(stacked, 'grp', axis=1, tiled=True)]
    ppermute x2 -> x0, starting transfers between devices: 6.42 us -> none  [the longest x1 4.5 us: extended(): before = lax.ppermute(last, axis, up)]
    unnamed x18, local copies, waits for them, and re-layouts: 0.65 us -> 6.01 us
    ppermute x2 -> x0, waiting for transfers between devices: 2.63 us -> none  [the longest x1 2.63 us: extended(): after = lax.ppermute(leading, axis, down)]
    another operation x2 -> x0, loops' own time: 2.63 us -> none  [the longest x1 2.6 us: per_device(): displacement, _ = lax.scan(one_entry, empty, listed)]
  transfers between devices with their start and end apart: 2 -> 0, of which waited for: 1 -> 0; matrix products, arithmetic and copies ran while one was open for 0% -> 0% of each run, Pallas kernels for 0% -> 0%
where the time goes in v1:
time: 85.8 us; the launch traced here: 85.2 us
  Pallas kernels  76.5 us (89%)
  local copies, waits for them, and re-layouts  7.37 us (9%)
  between operations  1.32 us (2%)
    pallas_call x1, Pallas kernels, per_device(): pl.pallas_call(functools.partial(kernel, blk, grp), out_shape=(shape, sha...  76.5 us
    unnamed x18, local copies, waits for them, and re-layouts  6.01 us

profile of v1, /device:TPU:1, one launch (start us, length us, event | category | flops | bytes accessed | tf_op | source)
XLA Modules:
  0.0 85.2 jit_solution(1964578931774088651)
XLA Ops:
  0.6 0.0 copy-start.5
  1.3 0.0 copy-start.6
  1.3 0.7 broadcast_in_dim.10.norm_prev
  2.0 0.0 copy-done.5
  2.0 0.0 copy-done.6
  2.0 0.0 copy-start
  2.0 0.7 copy-done
  2.8 0.0 copy-start.1
  2.8 0.7 copy-done.1
  3.5 0.0 copy-start.2
  3.5 0.7 copy-done.2
  4.2 0.0 copy-start.3
  4.2 0.7 copy-done.3
  4.9 0.0 copy-start.4
  4.9 0.7 copy-done.4
  5.6 76.5 %morph_step.1 = (f32[3,1024]{1,0:T(4,128)S(1)}, f32[3,1024]{1,0:T(4,128)S(1)}, f32[3,1024]{1,0:T(4,128)S(1)}, f32[3,128]{1,0:T(4,128)S(1)}, f32[3,1024]{1,0:T(4,128)S(1)}) custom-call(f32[3,1024]{1,0:T(4,128)S(1)} %copy-done, f32[3,1024]{1,0:T(4,128)S(1)} %copy-done.1, f32[3,1024]{1,0:T(4,128)S(1)} %copy-done.2, f32[3,1024]{1,0:T(4,128)S(1)} %copy-done.3, ...), custom_call_target="tpu_custom_call" | custom-call | flops 503316480 | bytes 1048576 | tf_op jit(solution)/shard_map/morph_step/pallas_call | solution.py:401
  82.1 0.6 slice_reduce_fusion
  82.8 0.6 copy.19
  83.4 0.6 copy.20
  84.0 0.6 copy.21
  84.6 0.6 copy.22
Async XLA Ops:
  0.6 1.4 %copy-start.5 = (f32[1024]{0:T(1024)S(1)}, f32[1024]{0:T(1024)}, u32[]{:S(2)}) copy-start(f32[1024]{0:T(1024)} %param.13) | copy-start | bytes 12292
  1.3 0.7 copy-start.6
  2.0 0.7 copy-start
  2.8 0.7 copy-start.1
  3.5 0.7 copy-start.2
  4.2 0.7 copy-start.3
  4.9 0.7 copy-start.4
